TPU v7x, 32 devices: a whole 2x2x4 slice. The times are simulated.
32 devices in a mesh: pair: 2 (over core), box: 4 (over y, x), tile: 4 (over z).
Axes of the slice: x: 2, y: 2, z: 4, core: 2. Of those that a mesh axis runs over, the one named last changes fastest.
Arguments:
- child_maps: bfloat16 [2, 16, 2304, 2304], P('pair', ('box', 'tile')), parts along dimension 1, as said below
- face_order: int32 [4, 2, 6], P('box'), parts along dimension 0, may hold values from 0 to 5, each once within a row
Outputs:
- parent_update: bfloat16 [2, 16, 1920, 1536], P('pair', ('box', 'tile')), parts along dimension 1
There are 4 independent parts, one for each index of `box`. A program takes and returns all parts, laid end to end along the dimension named above; each array names one. Nothing has to cross between parts.
Inputs may be any that keep to these rules, and one draw needn't show every extreme that they name: Each row of face_order lists every face once: entry 0 is the child's shared face, entries 1 to 5 its exterior faces in parent order. `child_maps`: child maps are dense with independent entries.
All inputs are finite; a program needn't handle non-finite values.
Results may differ from a plain program's by a relative error of at most 0.012.
Values may be sent and summed in bfloat16 or wider, within the bound.
A program may use at most 64 MiB of HBM per device.

v0:
```python
import math

import jax
import jax.numpy as jnp
from jax import lax
from jax.sharding import PartitionSpec as P

FACE = 768
FACES = 6
CF = 2
ITERS = 3


def from_partner(value, axis, distance):
    mask = 2**distance
    pairs = [(source, source ^ mask) for source in range(lax.axis_size(axis))]
    return lax.ppermute(value, axis, pairs)


def face_block(blocks, row_face, col_face):
    zero_start = jnp.zeros((), jnp.int32)
    piece_len = blocks.shape[1]
    start = (row_face, zero_start, col_face, zero_start)
    return lax.dynamic_slice(blocks, start, (1, piece_len, 1, piece_len)).reshape(
        piece_len, piece_len
    )


def assemble(gathered, tile_side, piece_len):
    return (
        gathered.reshape(tile_side, tile_side, piece_len, piece_len)
        .transpose(0, 2, 1, 3)
        .reshape(tile_side * piece_len, tile_side * piece_len)
    )


def product(left_matrix, right_matrix):
    result = jnp.dot(left_matrix, right_matrix, preferred_element_type=jnp.float32).astype(
        jnp.bfloat16
    )
    return result


def join_pair(stack, other, position, level):
    upper = position >> level & 1 == 1
    return jnp.where(
        upper, jnp.concatenate([other, stack], axis=0), jnp.concatenate([stack, other], axis=0)
    )


def local(child_maps, face_order):
    tile_side = math.isqrt(lax.axis_size("tile"))
    side_bits = tile_side.bit_length() - 1
    pair_index = lax.axis_index("pair")
    tile_index = lax.axis_index("tile")
    grid_row = tile_index // tile_side
    grid_col = tile_index % tile_side
    local_tile = child_maps[0, 0]
    piece_len = local_tile.shape[0] // FACES
    blocks = local_tile.reshape(FACES, piece_len, FACES, piece_len)
    face_list = lax.dynamic_index_in_dim(face_order[0], pair_index, 0, keepdims=False)
    own_face = face_list[0]
    own_shared = face_block(blocks, own_face, own_face)
    window = jnp.concatenate(
        [face_block(blocks, own_face, face_list[1 + number]) for number in range(CF)], axis=1
    )
    exterior = jnp.concatenate(
        [face_block(blocks, face_list[1 + number], own_face) for number in range(FACES - 1)], axis=0
    )
    mine_tiles = lax.all_gather(own_shared, "tile", axis=0, tiled=True)
    other_tiles = from_partner(mine_tiles, "pair", 0)
    shared_mine = assemble(mine_tiles, tile_side, piece_len)
    shared_other = assemble(other_tiles, tile_side, piece_len)
    column_stack = window[None]
    row_stack = exterior[None]
    for level in range(side_bits):
        column_other = from_partner(column_stack, "tile", side_bits + level)
        column_stack = join_pair(column_stack, column_other, grid_row, level)
        row_other = from_partner(row_stack, "tile", level)
        row_stack = join_pair(row_stack, row_other, grid_col, level)
    column_data = column_stack.reshape(tile_side * piece_len, CF * piece_len)
    row_data = row_stack.transpose(1, 0, 2).reshape(exterior.shape[0], tile_side * piece_len)
    powers = product(shared_mine, shared_other)
    series = column_data
    for sweep in range(ITERS):
        series = (
            series.astype(jnp.float32) + jnp.dot(powers, series, preferred_element_type=jnp.float32)
        ).astype(jnp.bfloat16)
        if sweep < ITERS - 1:
            powers = product(powers, powers)
    coupled = jnp.dot(shared_other, series, preferred_element_type=jnp.float32).astype(jnp.bfloat16)
    partner_series = from_partner(series, "pair", 0)
    left_half = jnp.where(pair_index == 0, coupled, partner_series)
    right_half = jnp.where(pair_index == 0, partner_series, coupled)
    factor = jnp.concatenate([left_half, right_half], axis=1)
    update = (
        jnp.dot(row_data, factor, preferred_element_type=jnp.float32) * math.sqrt(FACE)
    ).astype(jnp.bfloat16)
    return update[None, None]


def solution(mesh):
    return jax.shard_map(
        local,
        mesh=mesh,
        in_specs=(P("pair", ("box", "tile"), None, None), P("box", None, None)),
        out_specs=P("pair", ("box", "tile"), None, None),
        check_vma=False,
    )
```

profile of v0, /device:TPU:0, one launch (start us, length us, event | category | flops | bytes accessed | tf_op | source)
XLA Modules:
  0.0 162.9 jit_solution(4532696052220830217)
XLA Ops:
  6.5 0.0 copy-start
  6.5 0.0 all-gather.3.cloned.1.call-start
  6.5 0.7 copy-done
  7.2 0.7 fusion.6
  15.7 21.5 %reshape_squeeze.3 = bf16[6,384,6,384]{3,2,1,0:T(8,128)(2,1)} reshape(bf16[1,1,2304,2304]{3,2,1,0:T(8,128)(2,1)} %param.2) | data formatting | bytes 21233664 | tf_op jit(solution)/shard_map/reshape;squeeze | solution.py:60
  41.1 10.4 %constant_dynamic-slice_fusion.1 = (bf16[1,384,1,384]{3,2,1,0:T(2,128)(2,1)S(1)}, bf16[1,384,1,384]{3,2,1,0:T(2,128)(2,1)S(1)}, bf16[1,384,1,384]{3,2,1,0:T(2,12...) fusion(bf16[6,384,6,384]{3,2,1,0:T(8,128)(2,1)} %reshape_squeez, ...), kind=kLoop, calls=%fused_computation.26 | loop fusion | bytes 4718616 | tf_op jit(solution)/shard_map/dynamic_slice | solution.py:24
  51.5 0.8 copy.9
  52.3 0.0 all-gather.3.cloned.1.call-update
  52.4 0.1 copy_bitcast_fusion
  52.5 0.0 copy-start.2
  52.5 0.1 maximum_bitcast_fusion
  52.5 4.1 %collective-permute-start.2 = (bf16[1,384,768]{2,1,0:T(8,128)(2,1)S(1)}, bf16[1,384,768]{2,1,0:T(8,128)(2,1)}, u32[]{:S(2)}, u32[]{:S(2)}) collective-permute-start(bf16[1,384,768]{2,1,0:T(8,128)(2,1)S(1)} %maximum_bitcast_fusion), channel_id=1, source_target_pairs={{0,2},{1,3},{2,0},{3,1},{4,6},{5,7},{6,4},{7,5},{8,10},{9,11},{10,... | collective-permute-start | bytes 1769480 | tf_op jit(solution)/shard_map/ppermute | solution.py:17
  56.6 43.2 %all-gather.3.cloned.1.call-done = bf16[1,1536,1,384]{3,1,2,0:T(8,128)(2,1)} async-done(((bf16[1,384,1,384]{3,1,2,0:T(8,128)(2,1)}), bf16[1,1536,1,384]{3,1,2,0:T(8,128)(2,1)}) %all-gather.3.cloned.1.call-update) | async-done | bytes 1179664 | tf_op jit(solution)/shard_map/all_gather | solution.py:70
  99.9 0.1 collective-permute-start.1
  99.9 0.0 copy-done.2
  99.9 0.8 bitcast_dynamic-update-slice_fusion.4
  100.7 0.8 bitcast_dynamic-update-slice_fusion.3
  101.4 0.8 bitcast_dynamic-update-slice_fusion.2
  102.2 0.8 bitcast_dynamic-update-slice_fusion.1
  102.9 0.8 bitcast_dynamic-update-slice_fusion
  103.7 0.0 collective-permute-start
  103.7 0.0 copy-start.3
  103.7 0.0 collective-permute-done.2
  103.7 1.6 maximum_select_fusion.1
  105.3 0.1 copy-done.3
  105.3 1.2 copy.11
  106.5 0.2 copy.22
  106.8 0.0 collective-permute-done.1
  106.8 2.5 %copy.10 = bf16[2,2,384,384]{3,1,2,0:T(2,128)(2,1)S(1)} copy(bf16[2,2,384,384]{3,2,1,0:T(8,128)(2,1)} %bitcast.10) | data formatting | bytes 2359296 | tf_op jit(solution)/shard_map/reshape | solution.py:31
  109.3 0.2 copy.21
  109.5 0.0 copy-start.4
  109.5 1.1 convolution_convert_fusion.3
  110.6 0.0 copy-done.4
  110.6 1.1 convolution_convert_fusion.2
  111.7 1.1 fusion.7
  112.8 1.2 add_convert_fusion.1
  114.0 3.2 %add_convert_fusion = bf16[768,768]{1,0:T(8,128)(2,1)} fusion(bf16[768,768]{1,0:T(8,128)(2,1)S(1)} %add_convert_fusion.1, bf16[768,768]{1,0:T(8,128)(2,1)S(1)} %convolution_convert_fusion.2), kind=kOutput, calls=%fused_computation.7 | convolution fusion | flops 1814298624 | bytes 3538944 | tf_op jit(solution)/shard_map/dot_general | solution.py:87
  117.2 0.4 collective-permute-start.3
  117.6 21.0 %collective-permute-done = bf16[1,1920,384]{2,1,0:T(8,128)(2,1)} collective-permute-done((bf16[1,1920,384]{2,1,0:T(8,128)(2,1)}, bf16[1,1920,384]{2,1,0:T(8,128)(2,1)}, u32[]{:S(2)}, u32[]{:S(2)}) %collective-permute-start) | collective-permute-done | bytes 1474592 | tf_op jit(solution)/shard_map/ppermute | solution.py:17
  138.7 3.2 %fusion.1 = bf16[1920,2,384]{2,0,1:T(8,128)(2,1)S(1)} fusion(bf16[1,1920,384]{2,1,0:T(8,128)(2,1)} %bitcast.6, bf16[1,1920,384]{2,1,0:T(8,128)(2,1)} %collective-permute-done, pred[]{:T(512)S(6)} %eq.12), kind=kLoop, calls=%fused_computation.3 | loop fusion | flops 4423680 | bytes 5898241 | tf_op jit(solution)/shard_map/transpose | solution.py:82
  141.9 3.8 %copy.8 = bf16[1920,2,384]{0,2,1:T(8,128)(2,1)} copy(bf16[1920,2,384]{2,0,1:T(8,128)(2,1)S(1)} %fusion.1) | data formatting | bytes 5898240 | tf_op jit(solution)/shard_map/transpose | solution.py:82
  145.7 0.0 copy-start.1
  145.7 0.0 collective-permute-done.3
  145.7 3.2 %broadcast_select_fusion.1 = (bf16[768,768]{1,0:T(8,128)(2,1)S(1)}, bf16[768,768]{1,0:T(8,128)(2,1)S(1)}) fusion(bf16[768,768]{1,0:T(8,128)(2,1)} %collective-permute-done.3, pred[]{:T(512)S(6)} %eq.13, bf16[768,768]{1,0:T(8,128)(2,1)} %bitcast.64, bf16[768,768]{1,0:T(8,128)(2,1)} %add_convert_fusion), kind=kOutput, calls=%fused_computation.16 | convolution fusion | flops 907739136 | bytes 5898241 | tf_op jit(solution)/shard_map/dot_general | solution.py:91
  148.9 0.0 copy-done.1
  149.0 7.1 %fusion = bf16[1,1,1920,1536]{3,2,1,0:T(8,128)(2,1)} fusion(bf16[1920,768]{0,1:T(8,128)(2,1)S(1)} %bitcast.58, bf16[768,768]{1,0:T(8,128)(2,1)S(1)} %get-tuple-element.14, bf16[768,768]{1,0:T(8,128)(2,1)S(1)} %get-tuple-element.13), kind=kOutput, calls=%fused_computation.1 | convolution fusion | flops 4540465152 | bytes 11206656 | tf_op jit(solution)/shard_map/dot_general | solution.py:97
  (1 shorter events, 0.0 us)
Async XLA Ops:
  6.5 0.7 copy-start
  6.5 93.3 %all-gather.3.cloned.1.call-start = ((), (), s32[]{:S(2)}) async-start(), calls=%async_computation | async-start | bytes 1474560 | tf_op jit(solution)/shard_map/all_gather | solution.py:70
  52.5 47.5 %copy-start.2 = (bf16[1,384,1,384]{3,2,1,0:T(2,128)(2,1)S(1)}, bf16[1,384,1,384]{3,2,1,0:T(2,128)(2,1)}, u32[]{:S(2)}) copy-start(bf16[1,384,1,384]{3,2,1,0:T(2,128)(2,1)} %get-tuple-element.12) | copy-start | bytes 884740
  52.5 51.2 %collective-permute-start.2 = (bf16[1,384,768]{2,1,0:T(8,128)(2,1)S(1)}, bf16[1,384,768]{2,1,0:T(8,128)(2,1)}, u32[]{:S(2)}, u32[]{:S(2)}) collective-permute-start(bf16[1,384,768]{2,1,0:T(8,128)(2,1)S(1)} %maximum_bitcast_fusion), channel_id=1, source_target_pairs={{0,2},{1,3},{2,0},{3,1},{4,6},{5,7},{6,4},{7,5},{8,10},{9,11},{10,... | collective-permute-start | bytes 1769480 | tf_op jit(solution)/shard_map/ppermute | solution.py:17
  99.9 6.9 %collective-permute-start.1 = (bf16[1536,384]{1,0:T(8,128)(2,1)}, bf16[1536,384]{1,0:T(8,128)(2,1)}, u32[]{:S(2)}, u32[]{:S(2)}) collective-permute-start(bf16[1536,384]{1,0:T(8,128)(2,1)} %bitcast.61), channel_id=1, source_target_pairs={{0,16},{16,0},{1,17},{17,1},{2,18},{18,2},{3,19},{19,3},{4,20},{20... | collective-permute-start | bytes 3538952 | tf_op jit(solution)/shard_map/ppermute | solution.py:17
  103.7 35.0 %collective-permute-start = (bf16[1,1920,384]{2,1,0:T(8,128)(2,1)}, bf16[1,1920,384]{2,1,0:T(8,128)(2,1)}, u32[]{:S(2)}, u32[]{:S(2)}) collective-permute-start(bf16[1,1920,384]{2,1,0:T(8,128)(2,1)} %bitcast.6), channel_id=1, source_target_pairs={{0,1},{1,0},{2,3},{3,2},{4,5},{5,4},{6,7},{7,6},{8,9},{9,8},{10,11... | collective-permute-start | bytes 4423688 | tf_op jit(solution)/shard_map/ppermute | solution.py:17
  103.7 1.6 copy-start.3
  109.5 1.1 copy-start.4
  117.2 28.6 %collective-permute-start.3 = (bf16[768,768]{1,0:T(8,128)(2,1)}, bf16[768,768]{1,0:T(8,128)(2,1)}, u32[]{:S(2)}, u32[]{:S(2)}) collective-permute-start(bf16[768,768]{1,0:T(8,128)(2,1)} %add_convert_fusion), channel_id=1, source_target_pairs={{0,16},{16,0},{1,17},{17,1},{2,18},{18,2},{3,19},{19,3},{4,20},{20... | collective-permute-start | bytes 3538952 | tf_op jit(solution)/shard_map/ppermute | solution.py:17
  145.7 3.2 %copy-start.1 = (bf16[1920,2,384]{0,2,1:T(8,128)(2,1)S(1)}, bf16[1920,2,384]{0,2,1:T(8,128)(2,1)}, u32[]{:S(2)}) copy-start(bf16[1920,2,384]{0,2,1:T(8,128)(2,1)} %copy.8) | copy-start | bytes 8847364
Sparse Core Ops, SparseCore 0:
  52.5 47.3 all-gather.2
where the time goes:
time: 164 us; the launch traced here: 163 us
  waiting for transfers between devices  64.3 us (39%)
  local copies, waits for them, and re-layouts  46 us (28%)
  between operations  25.2 us (15%)
  matrix products  17.9 us (11%)
  other arithmetic  4.84 us (3%)
  starting transfers between devices  4.62 us (3%)
    all_gather x1, waiting for transfers between devices, local(): mine_tiles = lax.all_gather(own_shared, 'tile', axis=0, tiled=True)  43.2 us
    another operation x1, local copies, waits for them, and re-layouts, local(): blocks = local_tile.reshape(FACES, piece_len, FACES, piece_len)  21.5 us
    ppermute x4, waiting for transfers between devices, from_partner(): return lax.ppermute(value, axis, pairs)  21 us
    dynamic_slice x2, local copies, waits for them, and re-layouts, face_block(): lax.dynamic_slice(blocks, start, (1, piece_len, 1, piece_len))  11.2 us
    dot_general x1, matrix products, local(): jnp.dot(row_data, factor, preferred_element_type=jnp.float32)  7.08 us
    dot_general x3, matrix products, local(): jnp.dot(powers, series, preferred_element_type=jnp.float32)  5.43 us
    ppermute x4, starting transfers between devices, from_partner(): return lax.ppermute(value, axis, pairs)  4.61 us
    unnamed x17, local copies, waits for them, and re-layouts  4.32 us
  transfers between devices with their start and end apart: 5, of which 2 were waited for; matrix products, arithmetic and copies ran while one was open for 15% of the time, Pallas kernels for 0%

commit v1 on v0

v1 whole, which is shorter than its diff:
```python
import functools
import math

import jax
import jax.numpy as jnp
from jax import lax
from jax.experimental import pallas as pl
from jax.experimental.pallas import tpu as pltpu
from jax.sharding import PartitionSpec as P

FACE = 768
FACES = 6
CF = 2
ITERS = 3
MESH = pl.DeviceIdType.MESH
VMEM_LIMIT = 56 * 1024 * 1024


def extract_kernel(piece, order_ref, maps_ref, shared_ref, window_ref, exterior_ref, sems):
    child = lax.axis_index("pair")
    own = order_ref[0, child, 0]

    def block(row_face, col_face):
        rows = pl.ds(pl.multiple_of(row_face * piece, piece), piece)
        cols = pl.ds(pl.multiple_of(col_face * piece, piece), piece)
        return maps_ref.at[0, 0, rows, cols]

    copies = [pltpu.make_async_copy(block(own, own), shared_ref, sems.at[0])]
    for number in range(CF):
        copies.append(
            pltpu.make_async_copy(
                block(own, order_ref[0, child, 1 + number]),
                window_ref.at[:, pl.ds(number * piece, piece)],
                sems.at[1 + number],
            )
        )
    for number in range(FACES - 1):
        copies.append(
            pltpu.make_async_copy(
                block(order_ref[0, child, 1 + number], own),
                exterior_ref.at[pl.ds(number * piece, piece)],
                sems.at[1 + CF + number],
            )
        )
    for copy in copies:
        copy.start()
    for copy in copies:
        copy.wait()


def extract(child_maps, face_order, piece):
    shapes = ((piece, piece), (piece, CF * piece), ((FACES - 1) * piece, piece))
    if piece % 128 == 0:
        return pl.pallas_call(
            functools.partial(extract_kernel, piece),
            out_shape=[pltpu.VMEM(shape, child_maps.dtype) for shape in shapes],
            in_specs=[
                pl.BlockSpec(memory_space=pltpu.SMEM),
                pl.BlockSpec(memory_space=pltpu.HBM),
            ],
            out_specs=[pl.BlockSpec(memory_space=pltpu.VMEM)] * 3,
            scratch_shapes=[pltpu.SemaphoreType.DMA((CF + FACES,))],
            name="cut_faces",
        )(face_order, child_maps)
    faces = lax.dynamic_index_in_dim(face_order[0], lax.axis_index("pair"), 0, keepdims=False)
    tile = child_maps[0, 0]

    def block(row_face, col_face):
        return lax.dynamic_slice(tile, (row_face * piece, col_face * piece), (piece, piece))

    window = [block(faces[0], faces[1 + number]) for number in range(CF)]
    exterior = [block(faces[1 + number], faces[0]) for number in range(FACES - 1)]
    return (
        block(faces[0], faces[0]),
        jnp.concatenate(window, axis=1),
        jnp.concatenate(exterior, axis=0),
    )


def matmul(dst, left, right, rows, base=None):
    total = left.shape[0]

    @pl.loop(0, total // rows)
    def _(step):
        at = pl.ds(pl.multiple_of(step * rows, rows), rows)
        value = jnp.dot(left[at, :], right[...], preferred_element_type=jnp.float32)
        if base is not None:
            value = base[at, :].astype(jnp.float32) + value
        dst[at, :] = value.astype(dst.dtype)


def merge_kernel(
    side,
    piece,
    shared_ref,
    window_ref,
    exterior_ref,
    out_ref,
    mine,
    other,
    left,
    right,
    power,
    column,
    series,
    factor,
    rows_all,
    s_send,
    s_recv,
    w_send,
    w_recv,
    e_send,
    e_recv,
    f_send,
    f_recv,
    x_send,
    x_recv,
    l_sem,
):
    count = side * side
    faces = FACES - 1
    child = lax.axis_index("pair")
    tile = lax.axis_index("tile")
    grid_row = tile // side
    grid_col = lax.rem(tile, side)
    partner = {"pair": 1 - child}

    def peer(distance):
        return lax.rem(tile + distance, count)

    def row_peer(distance):
        return lax.rem(grid_row + distance, side)

    def col_peer(distance):
        return lax.rem(grid_col + distance, side)

    barrier = pltpu.get_barrier_semaphore()
    for distance in range(1, count):
        pl.semaphore_signal(
            barrier, inc=1, device_id={"tile": peer(distance)}, device_id_type=MESH
        )
    pl.semaphore_signal(barrier, inc=1, device_id=partner, device_id_type=MESH)
    pl.semaphore_wait(barrier, count)

    def remote(src, dst, send, recv, target):
        return pltpu.make_async_remote_copy(
            src_ref=src,
            dst_ref=dst,
            send_sem=send,
            recv_sem=recv,
            device_id=target,
            device_id_type=MESH,
        )

    s_copies = {}
    for distance in range(1, count):
        s_copies[distance] = remote(
            shared_ref,
            mine.at[tile],
            s_send.at[distance],
            s_recv.at[distance],
            {"tile": peer(distance)},
        )
    w_copies = {}
    for distance in range(1, side):
        w_copies[distance] = remote(
            window_ref,
            column.at[grid_row],
            w_send.at[distance],
            w_recv.at[distance],
            {"tile": row_peer(distance) * side + grid_col},
        )
    e_copies = {}
    for face in range(faces):
        for distance in range(1, side):
            e_copies[face, distance] = remote(
                exterior_ref.at[pl.ds(face * piece, piece)],
                rows_all.at[face, grid_col],
                e_send.at[face, distance],
                e_recv.at[face, distance],
                {"tile": grid_row * side + col_peer(distance)},
            )
    own_forward = remote(
        shared_ref, other.at[tile], f_send.at[0], f_recv.at[0], partner
    )
    for copy in s_copies.values():
        copy.start()
    own_forward.start()
    for copy in w_copies.values():
        copy.start()

    locals_ = [
        pltpu.make_async_copy(shared_ref, mine.at[tile], l_sem.at[0]),
        pltpu.make_async_copy(window_ref, column.at[grid_row], l_sem.at[1]),
    ]
    for face in range(faces):
        locals_.append(
            pltpu.make_async_copy(
                exterior_ref.at[pl.ds(face * piece, piece)],
                rows_all.at[face, grid_col],
                l_sem.at[2 + face],
            )
        )
    for copy in locals_:
        copy.start()

    forwards = [own_forward]
    for distance in range(1, count):
        s_copies[distance].wait_recv()
        source = lax.rem(tile + count - distance, count)
        forward = remote(
            mine.at[source],
            other.at[source],
            f_send.at[distance],
            f_recv.at[distance],
            partner,
        )
        forward.start()
        forwards.append(forward)
    for copy in e_copies.values():
        copy.start()
    for forward in forwards:
        forward.wait_recv()
    for copy in locals_:
        copy.wait()

    for number in range(count):
        at_row, at_col = number // side * piece, number % side * piece
        left[at_row : at_row + piece, at_col : at_col + piece] = mine[number]
        right[at_row : at_row + piece, at_col : at_col + piece] = other[number]

    block = math.gcd(left.shape[0], 256)
    matmul(power.at[0], left, right, block)
    for sweep in range(1, ITERS):
        matmul(power.at[sweep], power.at[sweep - 1], power.at[sweep - 1], block)
    for distance in range(1, side):
        w_copies[distance].wait_recv()
    for number in range(side):
        series[0, number * piece : (number + 1) * piece, :] = column[number]
    now = 0
    for sweep in range(ITERS):
        matmul(series.at[1 - now], power.at[sweep], series.at[now], block, base=series.at[now])
        now = 1 - now
    exchange = remote(series.at[now], factor.at[child], x_send, x_recv, partner)
    exchange.start()
    matmul(factor.at[child], right, series.at[now], block)
    exchange.wait_recv()

    half = CF * piece
    scale = math.sqrt(FACE)
    sub = 2
    step_rows = piece // sub
    for face in range(faces):
        for distance in range(1, side):
            e_copies[face, distance].wait_recv()

        @pl.loop(0, sub)
        def _(step, face=face):
            at = pl.ds(pl.multiple_of(step * step_rows, step_rows), step_rows)
            rows = jnp.concatenate([rows_all[face, k, at, :] for k in range(side)], axis=1)
            to = pl.ds(pl.multiple_of(face * piece + step * step_rows, step_rows), step_rows)
            for part in range(2):
                value = jnp.dot(rows, factor[part], preferred_element_type=jnp.float32) * scale
                out_ref[to, part * half : (part + 1) * half] = value.astype(out_ref.dtype)

    for copy in [*s_copies.values(), *w_copies.values(), *e_copies.values(), *forwards, exchange]:
        copy.wait_send()


def local(child_maps, face_order):
    side = math.isqrt(lax.axis_size("tile"))
    count = side * side
    piece = child_maps.shape[2] // FACES
    order = side * piece
    dtype = child_maps.dtype
    faces = FACES - 1
    shared, window, exterior = extract(child_maps, face_order, piece)
    dma = pltpu.SemaphoreType.DMA
    update = pl.pallas_call(
        functools.partial(merge_kernel, side, piece),
        out_shape=pltpu.VMEM((faces * piece, 2 * CF * piece), dtype),
        in_specs=[pl.BlockSpec(memory_space=pl.ANY)] * 3,
        out_specs=pl.BlockSpec(memory_space=pltpu.VMEM),
        scratch_shapes=[
            pltpu.VMEM((count, piece, piece), dtype),
            pltpu.VMEM((count, piece, piece), dtype),
            pltpu.VMEM((order, order), dtype),
            pltpu.VMEM((order, order), dtype),
            pltpu.VMEM((ITERS, order, order), dtype),
            pltpu.VMEM((side, piece, CF * piece), dtype),
            pltpu.VMEM((2, order, CF * piece), dtype),
            pltpu.VMEM((2, order, CF * piece), dtype),
            pltpu.VMEM((faces, side, piece, piece), dtype),
            dma((count,)),
            dma((count,)),
            dma((side,)),
            dma((side,)),
            dma((faces, side)),
            dma((faces, side)),
            dma((count,)),
            dma((count,)),
            dma(()),
            dma(()),
            dma((2 + faces,)),
        ],
        compiler_params=pltpu.CompilerParams(
            collective_id=0, has_side_effects=True, vmem_limit_bytes=VMEM_LIMIT
        ),
        name="merge",
    )(shared, window, exterior)
    return update[None, None]


def solution(mesh):
    return jax.shard_map(
        local,
        mesh=mesh,
        in_specs=(P("pair", ("box", "tile"), None, None), P("box", None, None)),
        out_specs=P("pair", ("box", "tile"), None, None),
        check_vma=False,
    )
```

time: 164 us -> 98 us (0.60)
  Pallas kernels: 0 us -> 92.6 us
  waiting for transfers between devices: 64.3 us -> 0 us
  local copies, waits for them, and re-layouts: 46 us -> 5.21 us
  between operations: 25.2 us -> 0.03 us
  matrix products: 17.9 us -> 0 us
  other arithmetic: 4.84 us -> 0 us
  starting transfers between devices: 4.62 us -> 0 us
    pallas_call x0 -> x2, Pallas kernels: none -> 92.6 us  [the longest x1 90.2 us: local(): pl.pallas_call(functools.partial(merge_kernel, side, piece), out_shape=pl...]
    all_gather x1 -> x0, waiting for transfers between devices: 43.2 us -> none  [local(): mine_tiles = lax.all_gather(own_shared, 'tile', axis=0, tiled=True)]
    another operation x1 -> x0, local copies, waits for them, and re-layouts: 21.5 us -> none  [local(): blocks = local_tile.reshape(FACES, piece_len, FACES, piece_len)]
    ppermute x4 -> x0, waiting for transfers between devices: 21 us -> none  [from_partner(): return lax.ppermute(value, axis, pairs)]
    dot_general x7 -> x0, matrix products: 17.9 us -> none  [the longest x1 7.08 us: local(): jnp.dot(row_data, factor, preferred_element_type=jnp.float32)]
    dynamic_slice x3 -> x0, local copies, waits for them, and re-layouts: 11.2 us -> none  [the longest x2 11.2 us: face_block(): lax.dynamic_slice(blocks, start, (1, piece_len, 1, piece_len))]
    transpose x2 -> x0, local copies, waits for them, and re-layouts: 5.04 us -> none  [the longest x1 3.82 us: local(): row_stack.transpose(1, 0, 2)]
    ppermute x4 -> x0, starting transfers between devices: 4.61 us -> none  [from_partner(): return lax.ppermute(value, axis, pairs)]
  transfers between devices with their start and end apart: 5 -> 0, of which waited for: 2 -> 0; matrix products, arithmetic and copies ran while one was open for 15% -> 0% of each run, Pallas kernels for 0% -> 0%
where the time goes in v1:
time: 98 us; the launch traced here: 97.8 us
  Pallas kernels  92.6 us (94%)
  local copies, waits for them, and re-layouts  5.21 us (5%)
    pallas_call x1, Pallas kernels, local(): pl.pallas_call(functools.partial(merge_kernel, side, piece), out_shape=pl...  90.2 us
    unnamed x7, local copies, waits for them, and re-layouts  5.21 us
    pallas_call x1, Pallas kernels, extract(): pl.pallas_call(functools.partial(extract_kernel, piece), out_shape=[pltpu...  2.4 us

profile of v1, /device:TPU:0, one launch (start us, length us, event | category | flops | bytes accessed | tf_op | source)
XLA Modules:
  0.0 97.8 jit_solution(17761880618167549932)
XLA Ops:
  0.0 2.4 %cut_faces.1 = (bf16[384,384]{1,0:T(8,128)(2,1)S(1)}, bf16[384,768]{1,0:T(8,128)(2,1)S(1)}, bf16[1920,384]{1,0:T(8,128)(2,1)S(1)}) custom-call(s32[1,2,6]{2,1,0:T(2,128)} %order_ref.1, bf16[1,1,2304,2304]{3,2,1,0:T(8,128)(2,1)} %maps_ref.1), custom_call_target="tpu_custom_call" | custom-call | tf_op jit(solution)/shard_map/cut_faces/pallas_call | solution.py:54
  2.4 0.0 copy-start
  2.4 1.1 %copy-done = bf16[1920,384]{1,0:T(8,128)(2,1)} copy-done((bf16[1920,384]{1,0:T(8,128)(2,1)}, bf16[1920,384]{1,0:T(8,128)(2,1)S(1)}, u32[]{:S(2)}) %copy-start) | copy-done | bytes 1474584
  3.5 0.0 copy-start.1
  3.5 0.8 copy-done.1
  4.3 0.0 copy-start.2
  4.3 0.7 copy-done.2
  5.1 90.2 %merge.1 = bf16[1920,1536]{1,0:T(8,128)(2,1)S(1)} custom-call(bf16[384,384]{1,0:T(8,128)(2,1)} %copy-done.2, bf16[384,768]{1,0:T(8,128)(2,1)} %copy-done.1, bf16[1920,384]{1,0:T(8,128)(2,1)} %copy-done), custom_call_target="tpu_custom_call" | custom-call | tf_op jit(solution)/shard_map/merge/pallas_call | solution.py:279
  95.3 2.6 %copy.4 = bf16[1,1,1920,1536]{3,2,1,0:T(8,128)(2,1)} copy(bf16[1,1,1920,1536]{3,2,1,0:T(8,128)(2,1)S(1)} %bitcast.1) | data formatting | bytes 11796480
Async XLA Ops:
  2.4 1.1 %copy-start = (bf16[1920,384]{1,0:T(8,128)(2,1)}, bf16[1920,384]{1,0:T(8,128)(2,1)S(1)}, u32[]{:S(2)}) copy-start(bf16[1920,384]{1,0:T(8,128)(2,1)S(1)} %get-tuple-element.10.exterior_ref) | copy-start | bytes 4423684
  3.5 0.8 copy-start.1
  4.3 0.7 copy-start.2

commit v2 on v1

--- a/solution.py
+++ b/solution.py
@@ -13,7 +13,7 @@
 CF = 2
 ITERS = 3
 MESH = pl.DeviceIdType.MESH
-VMEM_LIMIT = 56 * 1024 * 1024
+VMEM_LIMIT = 32 * 1024 * 1024
 
 
 def extract_kernel(piece, order_ref, maps_ref, shared_ref, window_ref, exterior_ref, sems):
@@ -188,6 +188,8 @@
     own_forward.start()
     for copy in w_copies.values():
         copy.start()
+    for copy in e_copies.values():
+        copy.start()
 
     locals_ = [
         pltpu.make_async_copy(shared_ref, mine.at[tile], l_sem.at[0]),
@@ -217,8 +219,6 @@
         )
         forward.start()
         forwards.append(forward)
-    for copy in e_copies.values():
-        copy.start()
     for forward in forwards:
         forward.wait_recv()
     for copy in locals_:

time: 98 us -> 76.1 us (0.78)
  Pallas kernels: 92.6 us -> 73.4 us
  local copies, waits for them, and re-layouts: 5.21 us -> 2.58 us
    pallas_call x1, Pallas kernels: 90.2 us -> 71 us  [local(): pl.pallas_call(functools.partial(merge_kernel, side, piece), out_shape=pl...]
    unnamed x7 -> x1, local copies, waits for them, and re-layouts: 5.21 us -> 2.58 us
where the time goes in v2:
time: 76.1 us; the launch traced here: 76 us
  Pallas kernels  73.4 us (96%)
  local copies, waits for them, and re-layouts  2.58 us (3%)
    pallas_call x1, Pallas kernels, local(): pl.pallas_call(functools.partial(merge_kernel, side, piece), out_shape=pl...  71 us
    unnamed x1, local copies, waits for them, and re-layouts  2.58 us
    pallas_call x1, Pallas kernels, extract(): pl.pallas_call(functools.partial(extract_kernel, piece), out_shape=[pltpu...  2.38 us

profile of v2, /device:TPU:0, one launch (start us, length us, event | category | flops | bytes accessed | tf_op | source)
XLA Modules:
  0.0 76.0 jit_solution(17291022158314540504)
XLA Ops:
  0.0 2.4 %cut_faces.1 = (bf16[384,384]{1,0:T(8,128)(2,1)S(1)}, bf16[384,768]{1,0:T(8,128)(2,1)S(1)}, bf16[1920,384]{1,0:T(8,128)(2,1)S(1)}) custom-call(s32[1,2,6]{2,1,0:T(2,128)} %order_ref.1, bf16[1,1,2304,2304]{3,2,1,0:T(8,128)(2,1)} %maps_ref.1), custom_call_target="tpu_custom_call" | custom-call | tf_op jit(solution)/shard_map/cut_faces/pallas_call | solution.py:54
  2.4 71.0 %merge.1 = bf16[1920,1536]{1,0:T(8,128)(2,1)S(1)} custom-call(bf16[384,384]{1,0:T(8,128)(2,1)S(1)} %get-tuple-element.8.shared_ref, bf16[384,768]{1,0:T(8,128)(2,1)S(1)} %get-tuple-element.9.window_ref, bf16[1920,384]{1,0:T(8,128)(2,1)S(1)} %get-tuple-element.10.exterior_ref), custom_call_target="tpu_custom_call" | custom-call | tf_op jit(solution)/shard_map/merge/pallas_call | solution.py:279
  73.4 2.6 %copy.4 = bf16[1,1,1920,1536]{3,2,1,0:T(8,128)(2,1)} copy(bf16[1,1,1920,1536]{3,2,1,0:T(8,128)(2,1)S(1)} %bitcast.1) | data formatting | bytes 11796480

commit v3 on v2

--- a/solution.py
+++ b/solution.py
@@ -14,6 +14,7 @@
 ITERS = 3
 MESH = pl.DeviceIdType.MESH
 VMEM_LIMIT = 32 * 1024 * 1024
+FINISH_LIMIT = 16 * 1024 * 1024
 
 
 def extract_kernel(piece, order_ref, maps_ref, shared_ref, window_ref, exterior_ref, sems):
@@ -89,6 +90,38 @@
         dst[at, :] = value.astype(dst.dtype)
 
 
+def final_rows(rows_ref, factor, dst, base, first, count):
+    half = factor.shape[2]
+    at = pl.ds(first, count)
+    rows = jnp.concatenate([rows_ref[k, at, :] for k in range(rows_ref.shape[0])], axis=1)
+    for part in range(2):
+        value = jnp.dot(rows, factor[part], preferred_element_type=jnp.float32)
+        value = value * math.sqrt(FACE)
+        dst[pl.ds(base + first, count), part * half : (part + 1) * half] = value.astype(dst.dtype)
+
+
+def finish_kernel(side, piece, held_ref, rows_ref, factor, out_ref, hold, sems):
+    parts = 2
+    size = piece // parts
+    start = held_ref.shape[0]
+    copies = []
+    for face in range(FACES - 2):
+        at = pl.ds(face * piece, piece)
+        copies.append(pltpu.make_async_copy(held_ref.at[at], out_ref.at[at], sems.at[parts + face]))
+        copies[-1].start()
+    for part in range(parts):
+        final_rows(rows_ref, factor, hold, 0, part * size, size)
+        copy = pltpu.make_async_copy(
+            hold.at[pl.ds(part * size, size)],
+            out_ref.at[pl.ds(start + part * size, size)],
+            sems.at[part],
+        )
+        copy.start()
+        copies.append(copy)
+    for copy in copies:
+        copy.wait()
+
+
 def merge_kernel(
     side,
     piece,
@@ -96,6 +129,8 @@
     window_ref,
     exterior_ref,
     out_ref,
+    rows_last,
+    factor,
     mine,
     other,
     left,
@@ -103,7 +138,6 @@
     power,
     column,
     series,
-    factor,
     rows_all,
     s_send,
     s_recv,
@@ -142,6 +176,9 @@
     pl.semaphore_signal(barrier, inc=1, device_id=partner, device_id_type=MESH)
     pl.semaphore_wait(barrier, count)
 
+    def rows_at(face):
+        return rows_all.at[face] if face < faces - 1 else rows_last
+
     def remote(src, dst, send, recv, target):
         return pltpu.make_async_remote_copy(
             src_ref=src,
@@ -175,7 +212,7 @@
         for distance in range(1, side):
             e_copies[face, distance] = remote(
                 exterior_ref.at[pl.ds(face * piece, piece)],
-                rows_all.at[face, grid_col],
+                rows_at(face).at[grid_col],
                 e_send.at[face, distance],
                 e_recv.at[face, distance],
                 {"tile": grid_row * side + col_peer(distance)},
@@ -199,7 +236,7 @@
         locals_.append(
             pltpu.make_async_copy(
                 exterior_ref.at[pl.ds(face * piece, piece)],
-                rows_all.at[face, grid_col],
+                rows_at(face).at[grid_col],
                 l_sem.at[2 + face],
             )
         )
@@ -246,22 +283,12 @@
     matmul(factor.at[child], right, series.at[now], block)
     exchange.wait_recv()
 
-    half = CF * piece
-    scale = math.sqrt(FACE)
-    sub = 2
-    step_rows = piece // sub
-    for face in range(faces):
+    for face in range(faces - 1):
         for distance in range(1, side):
             e_copies[face, distance].wait_recv()
-
-        @pl.loop(0, sub)
-        def _(step, face=face):
-            at = pl.ds(pl.multiple_of(step * step_rows, step_rows), step_rows)
-            rows = jnp.concatenate([rows_all[face, k, at, :] for k in range(side)], axis=1)
-            to = pl.ds(pl.multiple_of(face * piece + step * step_rows, step_rows), step_rows)
-            for part in range(2):
-                value = jnp.dot(rows, factor[part], preferred_element_type=jnp.float32) * scale
-                out_ref[to, part * half : (part + 1) * half] = value.astype(out_ref.dtype)
+        final_rows(rows_all.at[face], factor, out_ref, face * piece, 0, piece)
+    for distance in range(1, side):
+        e_copies[faces - 1, distance].wait_recv()
 
     for copy in [*s_copies.values(), *w_copies.values(), *e_copies.values(), *forwards, exchange]:
         copy.wait_send()
@@ -276,11 +303,19 @@
     faces = FACES - 1
     shared, window, exterior = extract(child_maps, face_order, piece)
     dma = pltpu.SemaphoreType.DMA
-    update = pl.pallas_call(
+    held, rows_last, factor = pl.pallas_call(
         functools.partial(merge_kernel, side, piece),
-        out_shape=pltpu.VMEM((faces * piece, 2 * CF * piece), dtype),
+        out_shape=[
+            pltpu.VMEM(((faces - 1) * piece, 2 * CF * piece), dtype),
+            pltpu.VMEM((side, piece, piece), dtype),
+            pltpu.VMEM((2, order, CF * piece), dtype),
+        ],
         in_specs=[pl.BlockSpec(memory_space=pl.ANY)] * 3,
-        out_specs=pl.BlockSpec(memory_space=pltpu.VMEM),
+        out_specs=[
+            pl.BlockSpec(memory_space=pltpu.VMEM),
+            pl.BlockSpec(memory_space=pltpu.VMEM),
+            pl.BlockSpec(memory_space=pltpu.VMEM),
+        ],
         scratch_shapes=[
             pltpu.VMEM((count, piece, piece), dtype),
             pltpu.VMEM((count, piece, piece), dtype),
@@ -289,8 +324,7 @@
             pltpu.VMEM((ITERS, order, order), dtype),
             pltpu.VMEM((side, piece, CF * piece), dtype),
             pltpu.VMEM((2, order, CF * piece), dtype),
-            pltpu.VMEM((2, order, CF * piece), dtype),
-            pltpu.VMEM((faces, side, piece, piece), dtype),
+            pltpu.VMEM((faces - 1, side, piece, piece), dtype),
             dma((count,)),
             dma((count,)),
             dma((side,)),
@@ -308,6 +342,22 @@
         ),
         name="merge",
     )(shared, window, exterior)
+    update = pl.pallas_call(
+        functools.partial(finish_kernel, side, piece),
+        out_shape=jax.ShapeDtypeStruct((faces * piece, 2 * CF * piece), dtype),
+        in_specs=[
+            pl.BlockSpec(memory_space=pl.ANY),
+            pl.BlockSpec(memory_space=pltpu.VMEM),
+            pl.BlockSpec(memory_space=pltpu.VMEM),
+        ],
+        out_specs=pl.BlockSpec(memory_space=pl.ANY),
+        scratch_shapes=[
+            pltpu.VMEM((piece, 2 * CF * piece), dtype),
+            dma((FACES,)),
+        ],
+        compiler_params=pltpu.CompilerParams(vmem_limit_bytes=FINISH_LIMIT),
+        name="finish",
+    )(held, rows_last, factor)
     return update[None, None]
 
 

time: 76.1 us -> 74.9 us (0.984)
  local copies, waits for them, and re-layouts: 2.58 us -> 0 us
  Pallas kernels: 73.4 us -> 74.7 us
    unnamed x1 -> x0, local copies, waits for them, and re-layouts: 2.58 us -> none
    pallas_call x1 -> x2, Pallas kernels: 71 us -> 72.3 us  [the longest x1 69.7 us: local(): pl.pallas_call(functools.partial(merge_kernel, side, piece), out_shape=[p...]
where the time goes in v3:
time: 74.9 us; the launch traced here: 74.7 us
  Pallas kernels  74.7 us (100%)
    pallas_call x1, Pallas kernels, local(): pl.pallas_call(functools.partial(merge_kernel, side, piece), out_shape=[p...  69.7 us
    pallas_call x1, Pallas kernels, local(): pl.pallas_call(functools.partial(finish_kernel, side, piece), out_shape=j...  2.62 us
    pallas_call x1, Pallas kernels, extract(): pl.pallas_call(functools.partial(extract_kernel, piece), out_shape=[pltpu...  2.38 us

profile of v3, /device:TPU:0, one launch (start us, length us, event | category | flops | bytes accessed | tf_op | source)
XLA Modules:
  0.0 74.7 jit_solution(534617679372054195)
XLA Ops:
  0.0 2.4 %cut_faces.1 = (bf16[384,384]{1,0:T(8,128)(2,1)S(1)}, bf16[384,768]{1,0:T(8,128)(2,1)S(1)}, bf16[1920,384]{1,0:T(8,128)(2,1)S(1)}) custom-call(s32[1,2,6]{2,1,0:T(2,128)} %order_ref.1, bf16[1,1,2304,2304]{3,2,1,0:T(8,128)(2,1)} %maps_ref.1), custom_call_target="tpu_custom_call" | custom-call | tf_op jit(solution)/shard_map/cut_faces/pallas_call | solution.py:55
  2.4 69.7 %merge.1 = (bf16[1536,1536]{1,0:T(8,128)(2,1)S(1)}, bf16[2,384,384]{2,1,0:T(8,128)(2,1)S(1)}, bf16[2,768,768]{2,1,0:T(8,128)(2,1)S(1)}) custom-call(bf16[384,384]{1,0:T(8,128)(2,1)S(1)} %get-tuple-element.11.shared_ref, bf16[384,768]{1,0:T(8,128)(2,1)S(1)} %get-tuple-element.12.window_ref, bf16[1920,384]{1,0:T(8,128)(2,1)S(1)} %get-tuple-element.13.exterior_ref), custom_call_target="tpu_custom_call" | custom-call | tf_op jit(solution)/shard_map/merge/pallas_call | solution.py:306
  72.1 2.6 %finish.1 = bf16[1920,1536]{1,0:T(8,128)(2,1)} custom-call(bf16[1536,1536]{1,0:T(8,128)(2,1)S(1)} %get-tuple-element.14.held_ref, bf16[2,384,384]{2,1,0:T(8,128)(2,1)S(1)} %get-tuple-element.15.rows_ref, bf16[2,768,768]{2,1,0:T(8,128)(2,1)S(1)} %get-tuple-element.16.factor), custom_call_target="tpu_custom_call" | custom-call | tf_op jit(solution)/shard_map/finish/pallas_call | solution.py:345

commit v4 on v3

--- a/solution.py
+++ b/solution.py
@@ -162,6 +162,14 @@
     def peer(distance):
         return lax.rem(tile + distance, count)
 
+    def grid_peer(distance):
+        row = lax.rem(grid_row + distance // side, side)
+        return row * side + lax.rem(grid_col + distance % side, side)
+
+    def grid_source(distance):
+        row = lax.rem(grid_row + side - distance // side, side)
+        return row * side + lax.rem(grid_col + side - distance % side, side)
+
     def row_peer(distance):
         return lax.rem(grid_row + distance, side)
 
@@ -196,7 +204,7 @@
             mine.at[tile],
             s_send.at[distance],
             s_recv.at[distance],
-            {"tile": peer(distance)},
+            {"tile": grid_peer(distance)},
         )
     w_copies = {}
     for distance in range(1, side):
@@ -246,7 +254,7 @@
     forwards = [own_forward]
     for distance in range(1, count):
         s_copies[distance].wait_recv()
-        source = lax.rem(tile + count - distance, count)
+        source = grid_source(distance)
         forward = remote(
             mine.at[source],
             other.at[source],

time: 74.9 us -> 74.9 us (level)
  no operation moved by 1% of the time
where the time goes in v4:
time: 74.9 us; the launch traced here: 74.7 us
  Pallas kernels  74.7 us (100%)
    pallas_call x1, Pallas kernels, local(): pl.pallas_call(functools.partial(merge_kernel, side, piece), out_shape=[p...  69.7 us
    pallas_call x1, Pallas kernels, local(): pl.pallas_call(functools.partial(finish_kernel, side, piece), out_shape=j...  2.62 us
    pallas_call x1, Pallas kernels, extract(): pl.pallas_call(functools.partial(extract_kernel, piece), out_shape=[pltpu...  2.39 us

profile of v4, /device:TPU:0, one launch (start us, length us, event | category | flops | bytes accessed | tf_op | source)
XLA Modules:
  0.0 74.7 jit_solution(1498180516623176536)
XLA Ops:
  0.0 2.4 %cut_faces.1 = (bf16[384,384]{1,0:T(8,128)(2,1)S(1)}, bf16[384,768]{1,0:T(8,128)(2,1)S(1)}, bf16[1920,384]{1,0:T(8,128)(2,1)S(1)}) custom-call(s32[1,2,6]{2,1,0:T(2,128)} %order_ref.1, bf16[1,1,2304,2304]{3,2,1,0:T(8,128)(2,1)} %maps_ref.1), custom_call_target="tpu_custom_call" | custom-call | tf_op jit(solution)/shard_map/cut_faces/pallas_call | solution.py:55
  2.4 69.7 %merge.1 = (bf16[1536,1536]{1,0:T(8,128)(2,1)S(1)}, bf16[2,384,384]{2,1,0:T(8,128)(2,1)S(1)}, bf16[2,768,768]{2,1,0:T(8,128)(2,1)S(1)}) custom-call(bf16[384,384]{1,0:T(8,128)(2,1)S(1)} %get-tuple-element.11.shared_ref, bf16[384,768]{1,0:T(8,128)(2,1)S(1)} %get-tuple-element.12.window_ref, bf16[1920,384]{1,0:T(8,128)(2,1)S(1)} %get-tuple-element.13.exterior_ref), custom_call_target="tpu_custom_call" | custom-call | tf_op jit(solution)/shard_map/merge/pallas_call | solution.py:314
  72.1 2.6 %finish.1 = bf16[1920,1536]{1,0:T(8,128)(2,1)} custom-call(bf16[1536,1536]{1,0:T(8,128)(2,1)S(1)} %get-tuple-element.14.held_ref, bf16[2,384,384]{2,1,0:T(8,128)(2,1)S(1)} %get-tuple-element.15.rows_ref, bf16[2,768,768]{2,1,0:T(8,128)(2,1)S(1)} %get-tuple-element.16.factor), custom_call_target="tpu_custom_call" | custom-call | tf_op jit(solution)/shard_map/finish/pallas_call | solution.py:353
